TPU v7x, 128 devices: a whole 4x4x4 slice. The times are simulated.
128 devices in a mesh: tok: 8 (over z, core), lat: 16 (over y, x).
Axes of the slice: x: 4, y: 4, z: 4, core: 2. Of those that a mesh axis runs over, the one named last changes fastest.
Arguments:
- activations: bfloat16 [2048, 2, 8192], P('lat', None, 'tok'), may hold values from -6 to 6
- enc_weight: bfloat16 [64, 2, 8192, 256], P('lat', None, 'tok'), may hold values from -0.046875 to 0.046875
- enc_bias: float32 [64, 256], P('lat'), may hold values from -3 to 3
- dec_weight: bfloat16 [64, 256, 2, 8192], P('lat', None, None, 'tok'), may hold values from -0.09375 to 0.09375
- dec_bias: float32 [2, 8192], P(None, 'tok'), may hold values from -3 to 3
- active: int32 [16, 16], replicated, may hold values from 0 to 63, all different within a row; in each aligned block of 16 rows (0 to 15, 16 to 31, ...) at most 8 rows name the same one
Outputs:
- grad_enc: bfloat16 [64, 2, 8192, 256], P('lat', None, 'tok')
- grad_enc_bias: float32 [64, 256], P('lat')
- grad_dec: bfloat16 [64, 256, 2, 8192], P('lat', None, None, 'tok')
- grad_dec_bias: float32 [2, 8192], P(None, 'tok')
Inputs may be any that keep to these rules, and one draw needn't show every extreme that they name: `active`: each row lists 16 different block ids; every block id appears in some row; no block id appears in more than 8 rows, and some block id appears in exactly 8 rows.
All inputs are finite; a program needn't handle non-finite values.
Results may differ from a plain program's by a relative error of at most 0.02.
Values may be sent and summed in bfloat16 or wider, within the bound.
A program may use at most 192 MiB of HBM per device.

v0:
```python
import math
import jax
import jax.numpy as jnp
from jax import lax
from jax.sharding import PartitionSpec as P

MOST = 8
TILE = 128
SPARSITY = 0.25
NORM_EPSILON = 1e-06


def slot_lists(active, first_block, block_count):
    tile_count = active.shape[0]
    block_ids = first_block + jnp.arange(block_count, dtype=jnp.int32)
    is_active = jnp.any(active[:, :, None] == block_ids[None, None, :], axis=1).astype(jnp.int32)
    rank_count = jnp.cumsum(is_active, axis=0)
    wanted = jnp.arange(MOST, dtype=jnp.int32) + 1
    picked = (is_active[:, :, None] == 1) & (rank_count[:, :, None] == wanted[None, None, :])
    tile_ids = jnp.arange(tile_count, dtype=jnp.int32)
    slot_tile = jnp.sum(jnp.where(picked, tile_ids[:, None, None], 0), axis=0)
    live_slot = jnp.any(picked, axis=0)
    return (slot_tile, live_slot)


def on_device(activations, enc_weight, enc_bias, dec_weight, dec_bias, active):
    slab_count = enc_weight.shape[0]
    tile_count = active.shape[0]
    tile_rows = activations.shape[0]
    models = activations.shape[1]
    feat_width = activations.shape[2]
    loss_scale = 1.0 / math.sqrt(MOST * TILE)
    first_block = lax.axis_index("lat") * slab_count
    slot_tile, live_slot = slot_lists(active, first_block, slab_count)
    live_mask = live_slot[:, :, None, None]
    gathered = lax.all_gather(activations, "lat", axis=0, tiled=True)
    tile_acts = gathered.reshape(tile_count, tile_rows, models, feat_width)
    chosen = tile_acts[slot_tile]
    pre_part = jnp.einsum(
        "smrad,sadj->smrj", chosen, enc_weight, preferred_element_type=jnp.float32
    )
    pre_act = lax.psum(pre_part, "tok") + enc_bias[:, None, None, :]
    features = jnp.where(live_mask, jnp.maximum(pre_act, 0.0), 0.0).astype(jnp.bfloat16)
    product = jnp.einsum(
        "smrj,sjad->smrad", features, dec_weight, preferred_element_type=jnp.float32
    )
    partial_value = (
        jnp.zeros((tile_count, tile_rows, models, feat_width), jnp.float32)
        .at[slot_tile]
        .add(product)
    )
    rounded = lax.optimization_barrier(partial_value.astype(jnp.bfloat16)).astype(jnp.float32)
    rounded = rounded.reshape(tile_count * tile_rows, models, feat_width)
    recon_mine = (
        lax.psum_scatter(
            rounded.astype(jnp.bfloat16), "lat", scatter_dimension=0, tiled=True
        ).astype(jnp.float32)
        + dec_bias[None, :, :]
    )
    error_mine = (recon_mine - activations.astype(jnp.float32)).astype(jnp.bfloat16)
    error_all = lax.all_gather(error_mine, "lat", axis=0, tiled=True)
    tile_err = error_all.reshape(tile_count, tile_rows, models, feat_width)
    err_chosen = tile_err[slot_tile]
    grad_part = jnp.einsum(
        "smrad,sjad->smrj", err_chosen, dec_weight, preferred_element_type=jnp.float32
    )
    dec_wide = dec_weight.astype(jnp.float32)
    squares = jnp.sum(jnp.square(dec_wide), axis=3)
    grad_sum, square_sum = (
        lax.psum(grad_part.astype(jnp.bfloat16), "tok").astype(jnp.float32),
        lax.psum(squares.astype(jnp.bfloat16), "tok").astype(jnp.float32),
    )
    dec_norms = jnp.sqrt(square_sum + NORM_EPSILON)
    feat_grad = loss_scale * (grad_sum + SPARSITY * jnp.sum(dec_norms, axis=2)[:, None, None, :])
    pre_grad = jnp.where(features > 0, feat_grad, 0.0).astype(jnp.bfloat16)
    grad_enc = jnp.einsum(
        "smrad,smrj->sadj", chosen, pre_grad, preferred_element_type=jnp.float32
    ).astype(jnp.bfloat16)
    grad_enc_bias = jnp.sum(pre_grad.astype(jnp.float32), axis=(1, 2))
    feat_total = jnp.sum(features.astype(jnp.float32), axis=(1, 2))
    recon_term = jnp.einsum(
        "smrj,smrad->sjad", features, err_chosen, preferred_element_type=jnp.float32
    )
    norm_term = SPARSITY * feat_total[:, :, None, None] * dec_wide / dec_norms[:, :, :, None]
    grad_dec = (loss_scale * (recon_term + norm_term)).astype(jnp.bfloat16)
    grad_dec_bias = loss_scale * jnp.sum(error_all.astype(jnp.float32), axis=0)
    return (grad_enc, grad_enc_bias, grad_dec, grad_dec_bias)


def solution(mesh):
    placed = (
        P("lat", None, "tok"),
        P("lat", None, "tok", None),
        P("lat", None),
        P("lat", None, None, "tok"),
        P(None, "tok"),
        P(),
    )
    return jax.shard_map(
        on_device,
        mesh=mesh,
        in_specs=placed,
        out_specs=(
            P("lat", None, "tok", None),
            P("lat", None),
            P("lat", None, None, "tok"),
            P(None, "tok"),
        ),
        check_vma=False,
    )
```

profile of v0, /device:TPU:0, one launch (start us, length us, event | category | flops | bytes accessed | tf_op | source)
XLA Modules:
  0.0 585.7 jit_solution(5982257089558291725)
XLA Ops:
  10.7 73.1 %all-gather.3.cloned.1.call-done = bf16[2048,2,1024]{2,0,1:T(8,128)(2,1)} async-done(((bf16[128,2,1024]{2,0,1:T(8,128)(2,1)}), bf16[2048,2,1024]{2,0,1:T(8,128)(2,1)}) %all-gather.3.cloned.1.call-update) | async-done | bytes 8388624 | tf_op jit(solution)/shard_map/all_gather | solution.py:36
  83.8 8.2 %copy.49 = bf16[16,128,2,1024]{3,1,2,0:T(8,128)(2,1)} copy(bf16[16,128,2,1024]{3,1,0,2:T(8,128)(2,1)} %bitcast.69) | data formatting | bytes 16777216 | tf_op jit(solution)/shard_map/reshape | solution.py:37
  92.0 10.6 %gather_fusion = bf16[32,128,2,1024]{3,1,2,0:T(8,128)(2,1)} fusion(bf16[16,128,2,1024]{3,1,2,0:T(8,128)(2,1)} %copy.49, s32[1024]{0:T(1024)S(1)} %pad_clamp_fusion), kind=kCustom, calls=%fused_computation | custom fusion | bytes 33554560 | tf_op jit(solution)/shard_map/gather | solution.py:38
  102.6 13.5 %fusion.11 = f32[4,8,128,256]{3,2,1,0:T(8,128)} fusion(bf16[4,8,128,2,1024]{4,2,3,1,0:T(8,128)(2,1)} %bitcast.65, bf16[4,2,1024,256]{3,2,1,0:T(8,128)(2,1)} %param.7), kind=kOutput, calls=%fused_computation.23 | convolution fusion | flops 4294967296 | bytes 25165824 | tf_op jit(solution)/shard_map/smrad,sadj->smrj/dot_general | solution.py:39
  116.6 72.3 %all-reduce.3.cloned.1.call-done = f32[4,8,128,256]{3,2,1,0:T(8,128)} async-done(((f32[4,8,128,256]{3,2,1,0:T(8,128)}), f32[4,8,128,256]{3,2,1,0:T(8,128)}) %all-reduce.3.cloned.1.call-update) | async-done | bytes 4194320 | tf_op jit(solution)/shard_map/psum | solution.py:42
  188.9 3.1 select_convert_fusion.1
  192.3 13.1 %fusion.9 = f32[4,8,128,2,1024]{4,2,3,1,0:T(8,128)} fusion(bf16[4,256,2,1024,1]{3,2,1,0,4:T(2,128)(2,1)S(1)} %bitcast.64, bf16[4,8,128,256]{3,2,1,0:T(8,128)(2,1)S(1)} %select_convert_fusion.1), kind=kOutput, calls=%fused_computation.21 | convolution fusion | flops 4294967296 | bytes 39845888 | tf_op jit(solution)/shard_map/smrj,sjad->smrad/dot_general | solution.py:44
  205.4 7.8 %broadcast_in_dim.28 = f32[16,128,2,1024]{3,1,2,0:T(8,128)} broadcast(f32[]{:T(128)} %constant.17.clone.1), dimensions={} | broadcast | bytes 16777220 | tf_op jit(solution)/shard_map/broadcast_in_dim | solution.py:48
  213.3 65.6 %scatter_fusion = f32[16,128,2,1024]{3,1,2,0:T(8,128)} fusion(f32[16,128,2,1024]{3,1,2,0:T(8,128)} %broadcast_in_dim.28, s32[32]{0:T(128)S(1)} %reshape.64, f32[32,128,2,1024]{3,1,2,0:T(8,128)} %bitcast.60), kind=kCustom, calls=%fused_computation.2 | custom fusion | flops 8388608 | bytes 100663424 | tf_op jit(solution)/shard_map/scatter-add | solution.py:50
  278.9 9.1 %convert_element_type.66 = bf16[16,128,2,1024]{3,1,2,0:T(8,128)(2,1)} convert(f32[16,128,2,1024]{3,1,2,0:T(8,128)} %scatter_fusion) | non-fusion elementwise | flops 4194304 | bytes 25165824 | tf_op jit(solution)/shard_map/convert_element_type | solution.py:52
  288.0 8.2 %copy.51 = bf16[16,128,2,1024]{3,1,0,2:T(8,128)(2,1)} copy(bf16[16,128,2,1024]{3,1,2,0:T(8,128)(2,1)} %convert_element_type.66) | data formatting | bytes 16777216 | tf_op jit(solution)/shard_map/optimization_barrier | solution.py:52
  296.2 84.8 %reduce-scatter.2.cloned.1.call-done = bf16[128,2,1024]{2,0,1:T(8,128)(2,1)} async-done(((bf16[2048,2,1024]{2,0,1:T(8,128)(2,1)}), bf16[128,2,1024]{2,0,1:T(8,128)(2,1)}) %reduce-scatter.2.cloned.1.call-update) | async-done | bytes 524304 | tf_op jit(solution)/shard_map/reduce_scatter | solution.py:55
  381.1 2.1 subtract_convert_fusion
  383.2 3.4 fusion
  386.6 13.9 %psum.23 = bf16[4,256,2]{1,2,0:T(2,128)(2,1)S(1)} all-reduce(bf16[4,256,2]{1,2,0:T(2,128)(2,1)S(1)} %fusion), channel_id=1, replica_groups=mesh['tok'=8,'lat'=16] {'tok'}, use_global_device_ids=true, to_apply=%region_9.10 | all-reduce | flops 2048 | bytes 8192 | tf_op jit(solution)/shard_map/psum | solution.py:71
  400.5 53.2 %all-gather.5.cloned.1.call-done = bf16[2048,2,1024]{2,0,1:T(8,128)(2,1)} async-done(((bf16[128,2,1024]{2,0,1:T(8,128)(2,1)}), bf16[2048,2,1024]{2,0,1:T(8,128)(2,1)}) %all-gather.5.cloned.1.call-update) | async-done | bytes 8388624 | tf_op jit(solution)/shard_map/all_gather | solution.py:61
  453.7 10.6 %gather_fusion.1 = bf16[32,128,2,1024]{3,1,2,0:T(8,128)(2,1)} fusion(bf16[16,128,2,1024]{3,1,0,2:T(8,128)(2,1)} %bitcast.61, s32[1024]{0:T(1024)S(1)} %pad_clamp_fusion), kind=kCustom, calls=%fused_computation.1 | custom fusion | bytes 33554560 | tf_op jit(solution)/shard_map/gather | solution.py:63
  464.4 12.8 %bitcast_convert_fusion.1 = bf16[4,8,128,256]{3,2,1,0:T(8,128)(2,1)} fusion(bf16[4,8,128,2,1024]{4,2,3,1,0:T(8,128)(2,1)} %bitcast.67, bf16[4,256,2,1024,1]{3,2,1,0,4:T(2,128)(2,1)} %bitcast.63), kind=kOutput, calls=%fused_computation.14 | convolution fusion | flops 4296015872 | bytes 23068672 | tf_op jit(solution)/shard_map/smrad,sjad->smrj/dot_general | solution.py:64
  477.3 5.0 convert_reduce_fusion
  482.9 60.1 %all-reduce.5.cloned.1.call-done = bf16[4,8,128,256]{3,2,1,0:T(8,128)(2,1)} async-done(((bf16[4,8,128,256]{3,2,1,0:T(8,128)(2,1)}), bf16[4,8,128,256]{3,2,1,0:T(8,128)(2,1)}) %all-reduce.5.cloned.1.call-update) | async-done | bytes 2097168 | tf_op jit(solution)/shard_map/psum | solution.py:70
  543.0 5.1 convert_reduce_fusion.1
  548.0 10.7 %fusion.4 = bf16[4,256,2,1024]{3,1,2,0:T(8,128)(2,1)} fusion(f32[4,256,2]{1,2,0:T(2,128)S(1)} %get-tuple-element.26, f32[4,256]{1,0:T(4,128)S(1)} %broadcast_multiply_fusion.1, bf16[4,256,2,1024]{3,2,1,0:T(2,128)(2,1)S(1)} %copy-done.1, bf16[4,8,128,2,1024]{4,2,3,1,0:T(8,128)(2,1)} %bitcast.68, bf16[4,8,128,256]{3,2,1,0:T(8,128)(2,1)S(1)} %select_convert_fusion.1), kind=kOutput, calls=%fused_computation.11 | convolution fusion | flops 4307550208 | bytes 27275264 | tf_op jit(solution)/shard_map/smrj,smrad->sjad/dot_general | solution.py:81
  558.7 8.7 %copy.58 = bf16[4,256,2,1024]{3,2,1,0:T(2,128)(2,1)} copy(bf16[4,256,2,1024]{3,1,2,0:T(8,128)(2,1)} %fusion.4) | data formatting | bytes 8388608
  567.4 11.8 %bitcast_convert_fusion = bf16[4,2,1024,256]{3,2,1,0:T(8,128)(2,1)} fusion(bf16[4,8,128,2,1024]{4,2,3,1,0:T(8,128)(2,1)} %bitcast.66, bf16[4,8,128,256]{3,2,1,0:T(8,128)(2,1)S(1)} %copy-done.2, bf16[4,8,128,256]{3,2,1,0:T(8,128)(2,1)S(1)} %select_convert_fusion.1, f32[4,256]{1,0:T(4,128)S(1)} %broadcast_multiply_fusion.2), kind=kOutput, calls=%fused_computation.10 | convolution fusion | flops 4303355904 | bytes 25169920 | tf_op jit(solution)/shard_map/smrad,smrj->sadj/dot_general | solution.py:76
  (39 shorter events, 5.1 us)
Async XLA Ops:
  7.2 76.7 %all-gather.3.cloned.1.call-start = ((), (), s32[]{:S(2)}) async-start(), calls=%async_computation.1 | async-start | bytes 8912896 | tf_op jit(solution)/shard_map/all_gather | solution.py:36
  9.2 179.7 %all-reduce.3.cloned.1.call-start = ((), (), s32[]{:S(2)}) async-start(), calls=%async_computation.2 | async-start | bytes 8388608 | tf_op jit(solution)/shard_map/psum | solution.py:42
  116.1 72.8 %copy-start.4 = (f32[4,256]{1,0:T(4,128)S(1)}, f32[4,256]{1,0:T(4,128)}, u32[]{:S(2)}) copy-start(f32[4,256]{1,0:T(4,128)} %param.8) | copy-start | bytes 12292
  116.1 265.0 %reduce-scatter.2.cloned.1.call-start = ((), (), s32[]{:S(2)}) async-start(), calls=%async_computation.3 | async-start | bytes 8912896 | tf_op jit(solution)/shard_map/reduce_scatter | solution.py:55
  188.9 3.4 copy-start
  296.2 84.9 %copy-start.3 = (bf16[128,2,1024]{2,1,0:T(2,128)(2,1)S(1)}, bf16[128,2,1024]{2,1,0:T(2,128)(2,1)}, u32[]{:S(2)}) copy-start(bf16[128,2,1024]{2,1,0:T(2,128)(2,1)} %param.6) | copy-start | bytes 1572868
  296.2 84.9 %copy-start.5 = (f32[2,1024]{1,0:T(2,128)S(1)}, f32[2,1024]{1,0:T(2,128)}, u32[]{:S(2)}) copy-start(f32[2,1024]{1,0:T(2,128)} %param.10) | copy-start | bytes 24580
  296.2 157.5 %all-gather.5.cloned.1.call-start = ((), (), s32[]{:S(2)}) async-start(), calls=%async_computation.4 | async-start | bytes 8912896 | tf_op jit(solution)/shard_map/all_gather | solution.py:61
  383.2 159.8 %all-reduce.5.cloned.1.call-start = ((), (), s32[]{:S(2)}) async-start(), calls=%async_computation.5 | async-start | bytes 4194304 | tf_op jit(solution)/shard_map/psum | solution.py:70
  543.0 5.1 copy-start.1
  558.7 8.7 %copy-start.2 = (bf16[4,8,128,256]{3,2,1,0:T(8,128)(2,1)S(1)}, bf16[4,8,128,256]{3,2,1,0:T(8,128)(2,1)}, u32[]{:S(2)}) copy-start(bf16[4,8,128,256]{3,2,1,0:T(8,128)(2,1)} %all-reduce.5.cloned.1.call-done) | copy-start | bytes 6291460
Sparse Core Ops, SparseCore 0:
  10.7 73.0 all-gather.2
  116.2 72.5 all-reduce.2
  296.3 84.7 reduce-scatter.1
  383.7 70.0 all-gather.4
  477.3 65.6 all-reduce.4
where the time goes:
time: 586 us
  waiting for transfers between devices  344 us (59%)
  other arithmetic  95.3 us (16%)
  matrix products  61.8 us (11%)
  local copies, waits for them, and re-layouts  56.7 us (10%)
  blocking collectives  13.9 us (2%)
  between operations  13.8 us (2%)
    reduce_scatter x1, waiting for transfers between devices, on_device(): lax.psum_scatter(rounded.astype(jnp.bfloat16), 'lat', scatter_dimension=0...  84.8 us
    all_gather x1, waiting for transfers between devices, on_device(): gathered = lax.all_gather(activations, 'lat', axis=0, tiled=True)  73.1 us
    psum x1, waiting for transfers between devices, on_device(): pre_act = lax.psum(pre_part, 'tok') + enc_bias[:, None, None, :]  72.3 us
    scatter-add x1, other arithmetic, on_device(): partial_value = jnp.zeros((tile_count, tile_rows, models, feat_width), jn...  65.6 us
    psum x1, waiting for transfers between devices, on_device(): lax.psum(grad_part.astype(jnp.bfloat16), 'tok').astype(jnp.float32)  60.1 us
    all_gather x1, waiting for transfers between devices, on_device(): error_all = lax.all_gather(error_mine, 'lat', axis=0, tiled=True)  53.2 us
    psum x1, blocking collectives, on_device(): lax.psum(squares.astype(jnp.bfloat16), 'tok').astype(jnp.float32)  13.9 us
    dot_general x1, matrix products, on_device(): jnp.einsum('smrad,sadj->smrj', chosen, enc_weight, preferred_element_type...  13.5 us
  transfers between devices with their start and end apart: 5, of which 5 were waited for; matrix products, arithmetic and copies ran while one was open for 2% of the time, Pallas kernels for 0%

commit v1 on v0

--- a/solution.py
+++ b/solution.py
@@ -39,7 +39,11 @@
     pre_part = jnp.einsum(
         "smrad,sadj->smrj", chosen, enc_weight, preferred_element_type=jnp.float32
     )
-    pre_act = lax.psum(pre_part, "tok") + enc_bias[:, None, None, :]
+
+    def detail_corner(load):
+        return jnp.sum(lax.all_gather(load, "tok"), 0)
+
+    pre_act = detail_corner(pre_part) + enc_bias[:, None, None, :]
     features = jnp.where(live_mask, jnp.maximum(pre_act, 0.0), 0.0).astype(jnp.bfloat16)
     product = jnp.einsum(
         "smrj,sjad->smrad", features, dec_weight, preferred_element_type=jnp.float32

time: 586 us -> 685 us (1.17)
  waiting for transfers between devices: 344 us -> 428 us
  other arithmetic: 95.3 us -> 110 us
    all_gather x0 -> x1, waiting for transfers between devices: none -> 155 us  [detail_corner(): return jnp.sum(lax.all_gather(load, 'tok'), 0)]
    psum x1 -> x0, waiting for transfers between devices: 72.3 us -> none  [on_device(): pre_act = lax.psum(pre_part, 'tok') + enc_bias[:, None, None, :]]
    reduce_sum x0 -> x1, other arithmetic: none -> 14.3 us  [detail_corner(): return jnp.sum(lax.all_gather(load, 'tok'), 0)]
where the time goes in v1:
time: 685 us; the launch traced here: 684 us
  waiting for transfers between devices  428 us (62%)
  other arithmetic  110 us (16%)
  matrix products  61.8 us (9%)
  local copies, waits for them, and re-layouts  56.7 us (8%)
  blocking collectives  13.8 us (2%)
  between operations  13.8 us (2%)
    all_gather x1, waiting for transfers between devices, detail_corner(): return jnp.sum(lax.all_gather(load, 'tok'), 0)  155 us
    reduce_scatter x1, waiting for transfers between devices, on_device(): lax.psum_scatter(rounded.astype(jnp.bfloat16), 'lat', scatter_dimension=0...  85.6 us
    all_gather x1, waiting for transfers between devices, on_device(): gathered = lax.all_gather(activations, 'lat', axis=0, tiled=True)  73.1 us
    scatter-add x1, other arithmetic, on_device(): partial_value = jnp.zeros((tile_count, tile_rows, models, feat_width), jn...  65.6 us
    psum x1, waiting for transfers between devices, on_device(): lax.psum(grad_part.astype(jnp.bfloat16), 'tok').astype(jnp.float32)  60.1 us
    all_gather x1, waiting for transfers between devices, on_device(): error_all = lax.all_gather(error_mine, 'lat', axis=0, tiled=True)  53.3 us
    reduce_sum x1, other arithmetic, detail_corner(): return jnp.sum(lax.all_gather(load, 'tok'), 0)  14.3 us
    psum x1, blocking collectives, on_device(): lax.psum(squares.astype(jnp.bfloat16), 'tok').astype(jnp.float32)  13.8 us
  transfers between devices with their start and end apart: 5, of which 5 were waited for; matrix products, arithmetic and copies ran while one was open for 2% of the time, Pallas kernels for 0%

profile of v1, /device:TPU:0, one launch (start us, length us, event | category | flops | bytes accessed | tf_op | source)
XLA Modules:
  0.0 684.0 jit_solution(8817741879537722139)
XLA Ops:
  10.7 73.1 %all-gather.5.cloned.1.call-done = bf16[2048,2,1024]{2,0,1:T(8,128)(2,1)} async-done(((bf16[128,2,1024]{2,0,1:T(8,128)(2,1)}), bf16[2048,2,1024]{2,0,1:T(8,128)(2,1)}) %all-gather.5.cloned.1.call-update) | async-done | bytes 8388624 | tf_op jit(solution)/shard_map/all_gather | solution.py:36
  83.8 8.2 %copy.60 = bf16[16,128,2,1024]{3,1,2,0:T(8,128)(2,1)} copy(bf16[16,128,2,1024]{3,1,0,2:T(8,128)(2,1)} %bitcast.71) | data formatting | bytes 16777216 | tf_op jit(solution)/shard_map/reshape | solution.py:37
  92.0 10.6 %gather_fusion = bf16[32,128,2,1024]{3,1,2,0:T(8,128)(2,1)} fusion(bf16[16,128,2,1024]{3,1,2,0:T(8,128)(2,1)} %copy.60, s32[1024]{0:T(1024)S(1)} %pad_clamp_fusion), kind=kCustom, calls=%fused_computation | custom fusion | bytes 33554560 | tf_op jit(solution)/shard_map/gather | solution.py:38
  102.6 13.5 %fusion.11 = f32[4,8,128,256]{3,2,1,0:T(8,128)} fusion(bf16[4,8,128,2,1024]{4,2,3,1,0:T(8,128)(2,1)} %bitcast.67, bf16[4,2,1024,256]{3,2,1,0:T(8,128)(2,1)} %param.7), kind=kOutput, calls=%fused_computation.23 | convolution fusion | flops 4294967296 | bytes 25165824 | tf_op jit(solution)/shard_map/smrad,sadj->smrj/dot_general | solution.py:39
  116.6 155.4 %all-gather.9.cloned.1.call-done = f32[32,8,128,256]{3,2,1,0:T(8,128)} async-done(((f32[4,8,128,256]{3,2,1,0:T(8,128)}), f32[32,8,128,256]{3,2,1,0:T(8,128)}) %all-gather.9.cloned.1.call-update) | async-done | bytes 33554448 | tf_op jit(solution)/shard_map/all_gather | solution.py:44
  272.0 14.3 %reduce_sum.67 = f32[4,8,128,256]{3,2,1,0:T(8,128)} reduce(f32[8,4,8,128,256]{4,3,2,1,0:T(8,128)} %bitcast.63, f32[]{:T(128)} %constant.17.clone.1), dimensions={0}, to_apply=%region_4.5 | reduce | flops 7340032 | bytes 37748740 | tf_op jit(solution)/shard_map/reduce_sum | solution.py:44
  286.3 3.1 select_convert_fusion.1
  289.8 13.1 %fusion.9 = f32[4,8,128,2,1024]{4,2,3,1,0:T(8,128)} fusion(bf16[4,256,2,1024,1]{3,2,1,0,4:T(2,128)(2,1)S(1)} %bitcast.66, bf16[4,8,128,256]{3,2,1,0:T(8,128)(2,1)S(1)} %select_convert_fusion.1), kind=kOutput, calls=%fused_computation.21 | convolution fusion | flops 4294967296 | bytes 39845888 | tf_op jit(solution)/shard_map/smrj,sjad->smrad/dot_general | solution.py:48
  302.9 7.8 %broadcast_in_dim.28 = f32[16,128,2,1024]{3,1,2,0:T(8,128)} broadcast(f32[]{:T(128)} %constant.17.clone.1), dimensions={} | broadcast | bytes 16777220 | tf_op jit(solution)/shard_map/broadcast_in_dim | solution.py:52
  310.8 65.6 %scatter_fusion = f32[16,128,2,1024]{3,1,2,0:T(8,128)} fusion(f32[16,128,2,1024]{3,1,2,0:T(8,128)} %broadcast_in_dim.28, s32[32]{0:T(128)S(1)} %reshape.64, f32[32,128,2,1024]{3,1,2,0:T(8,128)} %bitcast.61), kind=kCustom, calls=%fused_computation.2 | custom fusion | flops 8388608 | bytes 100663424 | tf_op jit(solution)/shard_map/scatter-add | solution.py:54
  376.4 9.1 %convert_element_type.66 = bf16[16,128,2,1024]{3,1,2,0:T(8,128)(2,1)} convert(f32[16,128,2,1024]{3,1,2,0:T(8,128)} %scatter_fusion) | non-fusion elementwise | flops 4194304 | bytes 25165824 | tf_op jit(solution)/shard_map/convert_element_type | solution.py:56
  385.5 8.2 %copy.62 = bf16[16,128,2,1024]{3,1,0,2:T(8,128)(2,1)} copy(bf16[16,128,2,1024]{3,1,2,0:T(8,128)(2,1)} %convert_element_type.66) | data formatting | bytes 16777216 | tf_op jit(solution)/shard_map/optimization_barrier | solution.py:56
  393.7 85.6 %reduce-scatter.2.cloned.1.call-done = bf16[128,2,1024]{2,0,1:T(8,128)(2,1)} async-done(((bf16[2048,2,1024]{2,0,1:T(8,128)(2,1)}), bf16[128,2,1024]{2,0,1:T(8,128)(2,1)}) %reduce-scatter.2.cloned.1.call-update) | async-done | bytes 524304 | tf_op jit(solution)/shard_map/reduce_scatter | solution.py:59
  481.5 3.4 fusion
  484.9 13.8 %psum.15 = bf16[4,256,2]{1,2,0:T(2,128)(2,1)S(1)} all-reduce(bf16[4,256,2]{1,2,0:T(2,128)(2,1)S(1)} %fusion), channel_id=1, replica_groups=mesh['tok'=8,'lat'=16] {'tok'}, use_global_device_ids=true, to_apply=%region_9.10 | all-reduce | flops 2048 | bytes 8192 | tf_op jit(solution)/shard_map/psum | solution.py:75
  498.7 53.3 %all-gather.7.cloned.1.call-done = bf16[2048,2,1024]{2,0,1:T(8,128)(2,1)} async-done(((bf16[128,2,1024]{2,0,1:T(8,128)(2,1)}), bf16[2048,2,1024]{2,0,1:T(8,128)(2,1)}) %all-gather.7.cloned.1.call-update) | async-done | bytes 8388624 | tf_op jit(solution)/shard_map/all_gather | solution.py:65
  552.0 10.6 %gather_fusion.1 = bf16[32,128,2,1024]{3,1,2,0:T(8,128)(2,1)} fusion(bf16[16,128,2,1024]{3,1,0,2:T(8,128)(2,1)} %bitcast.62, s32[1024]{0:T(1024)S(1)} %pad_clamp_fusion), kind=kCustom, calls=%fused_computation.1 | custom fusion | bytes 33554560 | tf_op jit(solution)/shard_map/gather | solution.py:67
  562.6 12.8 %bitcast_convert_fusion.1 = bf16[4,8,128,256]{3,2,1,0:T(8,128)(2,1)} fusion(bf16[4,8,128,2,1024]{4,2,3,1,0:T(8,128)(2,1)} %bitcast.69, bf16[4,256,2,1024,1]{3,2,1,0,4:T(2,128)(2,1)} %bitcast.65), kind=kOutput, calls=%fused_computation.14 | convolution fusion | flops 4296015872 | bytes 23068672 | tf_op jit(solution)/shard_map/smrad,sjad->smrj/dot_general | solution.py:68
  575.5 5.0 convert_reduce_fusion
  581.1 60.1 %all-reduce.2.cloned.1.call-done = bf16[4,8,128,256]{3,2,1,0:T(8,128)(2,1)} async-done(((bf16[4,8,128,256]{3,2,1,0:T(8,128)(2,1)}), bf16[4,8,128,256]{3,2,1,0:T(8,128)(2,1)}) %all-reduce.2.cloned.1.call-update) | async-done | bytes 2097168 | tf_op jit(solution)/shard_map/psum | solution.py:74
  641.2 5.1 convert_reduce_fusion.1
  646.3 10.7 %fusion.4 = bf16[4,256,2,1024]{3,1,2,0:T(8,128)(2,1)} fusion(f32[4,256,2]{1,2,0:T(2,128)S(1)} %get-tuple-element.30, f32[4,256]{1,0:T(4,128)S(1)} %broadcast_multiply_fusion.1, bf16[4,256,2,1024]{3,2,1,0:T(2,128)(2,1)S(1)} %copy-done.1, bf16[4,8,128,2,1024]{4,2,3,1,0:T(8,128)(2,1)} %bitcast.70, bf16[4,8,128,256]{3,2,1,0:T(8,128)(2,1)S(1)} %select_convert_fusion.1), kind=kOutput, calls=%fused_computation.11 | convolution fusion | flops 4307550208 | bytes 27275264 | tf_op jit(solution)/shard_map/smrj,smrad->sjad/dot_general | solution.py:85
  657.0 8.7 %copy.69 = bf16[4,256,2,1024]{3,2,1,0:T(2,128)(2,1)} copy(bf16[4,256,2,1024]{3,1,2,0:T(8,128)(2,1)} %fusion.4) | data formatting | bytes 8388608
  665.7 11.8 %bitcast_convert_fusion = bf16[4,2,1024,256]{3,2,1,0:T(8,128)(2,1)} fusion(bf16[4,8,128,2,1024]{4,2,3,1,0:T(8,128)(2,1)} %bitcast.68, bf16[4,8,128,256]{3,2,1,0:T(8,128)(2,1)S(1)} %copy-done.2, bf16[4,8,128,256]{3,2,1,0:T(8,128)(2,1)S(1)} %select_convert_fusion.1, f32[4,256]{1,0:T(4,128)S(1)} %broadcast_multiply_fusion.2), kind=kOutput, calls=%fused_computation.10 | convolution fusion | flops 4303355904 | bytes 25169920 | tf_op jit(solution)/shard_map/smrad,smrj->sadj/dot_general | solution.py:80
  (40 shorter events, 7.2 us)
Async XLA Ops:
  7.2 76.7 %all-gather.5.cloned.1.call-start = ((), (), s32[]{:S(2)}) async-start(), calls=%async_computation.1 | async-start | bytes 8912896 | tf_op jit(solution)/shard_map/all_gather | solution.py:36
  9.2 262.8 %all-gather.9.cloned.1.call-start = ((), (), s32[]{:S(2)}) async-start(), calls=%async_computation.5 | async-start | bytes 37748736 | tf_op jit(solution)/shard_map/all_gather | solution.py:44
  116.1 363.2 %reduce-scatter.2.cloned.1.call-start = ((), (), s32[]{:S(2)}) async-start(), calls=%async_computation.2 | async-start | bytes 8912896 | tf_op jit(solution)/shard_map/reduce_scatter | solution.py:59
  272.0 14.4 %copy-start.4 = (f32[4,256]{1,0:T(4,128)S(1)}, f32[4,256]{1,0:T(4,128)}, u32[]{:S(2)}) copy-start(f32[4,256]{1,0:T(4,128)} %param.8) | copy-start | bytes 12292
  286.3 3.4 copy-start
  393.6 85.7 %copy-start.3 = (bf16[128,2,1024]{2,1,0:T(2,128)(2,1)S(1)}, bf16[128,2,1024]{2,1,0:T(2,128)(2,1)}, u32[]{:S(2)}) copy-start(bf16[128,2,1024]{2,1,0:T(2,128)(2,1)} %param.6) | copy-start | bytes 1572868
  393.6 85.7 %copy-start.5 = (f32[2,1024]{1,0:T(2,128)S(1)}, f32[2,1024]{1,0:T(2,128)}, u32[]{:S(2)}) copy-start(f32[2,1024]{1,0:T(2,128)} %param.10) | copy-start | bytes 24580
  393.7 158.3 %all-gather.7.cloned.1.call-start = ((), (), s32[]{:S(2)}) async-start(), calls=%async_computation.3 | async-start | bytes 8912896 | tf_op jit(solution)/shard_map/all_gather | solution.py:65
  481.5 159.8 %all-reduce.2.cloned.1.call-start = ((), (), s32[]{:S(2)}) async-start(), calls=%async_computation.4 | async-start | bytes 4194304 | tf_op jit(solution)/shard_map/psum | solution.py:74
  641.2 5.1 copy-start.1
  657.0 8.7 %copy-start.2 = (bf16[4,8,128,256]{3,2,1,0:T(8,128)(2,1)S(1)}, bf16[4,8,128,256]{3,2,1,0:T(8,128)(2,1)}, u32[]{:S(2)}) copy-start(bf16[4,8,128,256]{3,2,1,0:T(8,128)(2,1)} %all-reduce.2.cloned.1.call-done) | copy-start | bytes 6291460
Sparse Core Ops, SparseCore 0:
  10.7 73.0 all-gather.4
  116.2 155.6 all-gather.8
  393.8 85.5 reduce-scatter.1
  481.9 69.9 all-gather.6
  575.6 65.6 all-reduce.1
